TPU v7x, 32 devices: a whole 2x2x4 slice. The times are simulated.
32 devices in a mesh: row: 4 (over y, core), col: 8 (over z, x).
Axes of the slice: x: 2, y: 2, z: 4, core: 2. Of those that a mesh axis runs over, the one named last changes fastest.
Arguments:
- amplitudes: bfloat16 [4096, 2048], P('row', 'col'), may hold values from -6 to 6
- drive: float32 [4096, 2048], P('row', 'col'), may hold values from -6 to 6
- pair_irrep: int32 [2048], replicated, may hold values from 0 to 7, as said below
- occ_irrep: int32 [4096], replicated, may hold values from 0 to 7
- ladder_ints: bfloat16 [2048, 2048], P('row', 'col'), may hold values from -0.375 to 0.375
- hole_ints: bfloat16 [4096, 4096], P('row'), may hold values from -0.25 to 0.25, as said below
- occ_energy: float32 [64], replicated, may hold values from -1.5 to -0.5
- pair_energy: float32 [2048], P('col'), may hold values from 1 to 3
Outputs:
- residual: float32 [4096, 2048], P('row', 'col')
- updated: bfloat16 [4096, 2048], P('row', 'col')
Inputs may be any that keep to these rules, and one draw needn't show every extreme that they name: hole_ints is symmetric: hole_ints[ij, kl] == hole_ints[kl, ij]. `pair_irrep`: any irrep may hold any share of the virtual pairs, all of them included.
All inputs are finite; a program needn't handle non-finite values.
Results may differ from a plain program's by a relative error of at most 0.001.
Values may be sent and summed in bfloat16 or wider, within the bound.
A program may use at most 64 MiB of HBM per device.

v0:
```python
import jax
import jax.numpy as jnp
from jax import lax
from jax.sharding import PartitionSpec as P


def body(amplitudes, drive, pair_irrep, occ_irrep, ladder_ints, hole_ints, occ_energy, pair_energy):
    row_rank = lax.axis_index("row")
    col_rank = lax.axis_index("col")
    occ_rows = amplitudes.shape[0]
    pair_cols = amplitudes.shape[1]
    ladder_rows = ladder_ints.shape[0]
    own_pairs = lax.dynamic_slice_in_dim(pair_irrep, col_rank * pair_cols, pair_cols)
    ladder_labels = lax.dynamic_slice_in_dim(pair_irrep, row_rank * ladder_rows, ladder_rows)
    own_occ = lax.dynamic_slice_in_dim(occ_irrep, row_rank * occ_rows, occ_rows)
    ladder_kept = jnp.where(
        ladder_labels[:, None] == own_pairs[None, :], ladder_ints, jnp.zeros_like(ladder_ints)
    )
    ladder_full = lax.all_gather(ladder_kept, "row", axis=0, tiled=True)
    particle = jnp.dot(
        lax.all_gather(amplitudes, "col", axis=1, tiled=True),
        ladder_full,
        preferred_element_type=jnp.float32,
    )
    hole_kept = jnp.where(
        own_occ[:, None] == occ_irrep[None, :], hole_ints, jnp.zeros_like(hole_ints)
    )
    hole_part = lax.psum_scatter(
        lax.dot_general(
            hole_kept, amplitudes, (((0,), (0,)), ((), ())), preferred_element_type=jnp.float32
        ),
        "row",
        scatter_dimension=0,
        tiled=True,
    )
    residual = drive + particle + hole_part
    pair_occ = (occ_energy[:, None] + occ_energy[None, :]).reshape(-1)
    own_energy = lax.dynamic_slice_in_dim(pair_occ, row_rank * occ_rows, occ_rows)
    denominator = pair_energy[None, :] - own_energy[:, None]
    updated = (amplitudes.astype(jnp.float32) - residual / denominator).astype(jnp.bfloat16)
    return (residual, updated)


def solution(mesh):
    in_specs = (
        P("row", "col"),
        P("row", "col"),
        P(),
        P(),
        P("row", "col"),
        P("row", None),
        P(),
        P("col"),
    )
    out_specs = (P("row", "col"), P("row", "col"))
    return jax.shard_map(body, mesh=mesh, in_specs=in_specs, out_specs=out_specs, check_vma=False)
```

profile of v0, /device:TPU:0, one launch (start us, length us, event | category | flops | bytes accessed | tf_op | source)
XLA Modules:
  0.0 165.6 jit_solution(14204794873492175152)
XLA Ops:
  7.2 0.0 all-gather.3.cloned.1.call-start
  7.2 0.8 dynamic_slice.12
  8.0 0.8 dynamic_slice.13
  8.7 1.8 %compare_select_fusion.2 = bf16[512,256]{1,0:T(8,128)(2,1)} fusion(bf16[512,256]{1,0:T(8,128)(2,1)} %param.12, s32[256]{0:T(256)S(1)} %dynamic_slice.13, s32[512]{0:T(512)S(1)} %dynamic_slice.12), kind=kLoop, calls=%fused_computation.9 | loop fusion | flops 262144 | bytes 527360 | tf_op jit(solution)/shard_map/jit(_where)/select_n | solution.py:16
  10.5 0.0 all-gather.3.cloned.1.call-update
  10.6 0.0 all-gather.5.cloned.1.call-start
  10.6 0.7 all-gather.5.cloned.1.call-update
  11.3 0.0 reduce-scatter.2.cloned.1.call-start
  11.4 0.7 dynamic_slice.14
  12.1 8.5 %fusion = f32[4096,256]{0,1:T(8,128)} fusion(bf16[1024,256]{1,0:T(8,128)(2,1)} %param.8, bf16[1024,4096]{1,0:T(8,128)(2,1)} %param.13, s32[4096]{0:T(1024)} %param.11, s32[1024]{0:T(1024)S(1)} %dynamic_slice.14), kind=kOutput, calls=%fused_computation.1 | convolution fusion | flops 2155872256 | bytes 13127680 | tf_op jit(solution)/shard_map/dot_general | solution.py:29
  20.6 0.0 reduce-scatter.2.cloned.1.call-update
  20.6 0.0 copy-done
  20.6 0.2 copy.12
  20.8 0.0 copy-done.2
  20.8 0.1 broadcast_add_fusion
  20.9 0.1 add.43
  21.0 0.0 copy-done.1
  21.0 0.3 copy.10
  21.3 8.8 %all-gather.3.cloned.1.call-done = bf16[2048,256]{1,0:T(8,128)(2,1)} async-done(((bf16[512,256]{1,0:T(8,128)(2,1)}), bf16[2048,256]{1,0:T(8,128)(2,1)}) %all-gather.3.cloned.1.call-update) | async-done | bytes 1048592 | tf_op jit(solution)/shard_map/all_gather | solution.py:19
  30.1 77.1 %all-gather.5.cloned.1.call-done = bf16[1024,2048]{1,0:T(8,128)(2,1)} async-done(((bf16[1024,256]{1,0:T(8,128)(2,1)}), bf16[1024,2048]{1,0:T(8,128)(2,1)}) %all-gather.5.cloned.1.call-update) | async-done | bytes 4194320 | tf_op jit(solution)/shard_map/all_gather | solution.py:21
  107.2 45.2 %reduce-scatter.2.cloned.1.call-done = f32[1024,256]{0,1:T(8,128)} async-done(((f32[4096,256]{0,1:T(8,128)}), f32[1024,256]{0,1:T(8,128)}) %reduce-scatter.2.cloned.1.call-update) | async-done | bytes 1048592 | tf_op jit(solution)/shard_map/reduce_scatter | solution.py:28
  152.5 4.3 %subtract_convert_fusion = (bf16[1024,256]{0,1:T(8,128)(2,1)S(1)}, f32[1024,256]{0,1:T(8,128)S(1)}) fusion(bf16[1024,256]{0,1:T(8,128)(2,1)S(1)} %copy.12, f32[1024]{0:T(1024)S(1)} %dynamic_slice.15, f32[256]{0:T(256)S(1)} %copy-done.3, f32[1024,256]{0,1:T(8,128)} %reduce-scatter.2.cloned.1.call-done, f32[1024,256]{0,1:T(8,128)S(1)} %copy.10, ...), kind=kOutput, calls=%fused_computation.8 | convolution fusion | flops 1075576832 | bytes 9442304 | tf_op jit(solution)/shard_map/dot_general | solution.py:20
  156.8 1.3 copy.13
  158.1 1.0 copy.14
  (6 shorter events, 0.0 us)
Async XLA Ops:
  7.2 23.0 %all-gather.3.cloned.1.call-start = ((), (), s32[]{:S(2)}) async-start(), calls=%async_computation.1 | async-start | bytes 1310720 | tf_op jit(solution)/shard_map/all_gather | solution.py:19
  10.6 96.7 %all-gather.5.cloned.1.call-start = ((), (), s32[]{:S(2)}) async-start(), calls=%async_computation.2 | async-start | bytes 4718592 | tf_op jit(solution)/shard_map/all_gather | solution.py:21
  11.3 141.2 %reduce-scatter.2.cloned.1.call-start = ((), (), s32[]{:S(2)}) async-start(), calls=%async_computation.3 | async-start | bytes 5242880 | tf_op jit(solution)/shard_map/reduce_scatter | solution.py:28
  12.1 8.5 %copy-start = (bf16[1024,256]{1,0:T(8,128)(2,1)S(1)}, bf16[1024,256]{1,0:T(8,128)(2,1)}, u32[]{:S(2)}) copy-start(bf16[1024,256]{1,0:T(8,128)(2,1)} %param.8) | copy-start | bytes 1572868
  12.1 8.8 %copy-start.2 = (f32[64]{0:T(128)S(1)}, f32[64]{0:T(128)}, u32[]{:S(2)}) copy-start(f32[64]{0:T(128)} %param.14) | copy-start | bytes 772
  12.1 8.9 %copy-start.1 = (f32[1024,256]{1,0:T(8,128)S(1)}, f32[1024,256]{1,0:T(8,128)}, u32[]{:S(2)}) copy-start(f32[1024,256]{1,0:T(8,128)} %param.9) | copy-start | bytes 3145732
  12.1 140.4 %copy-start.3 = (f32[256]{0:T(256)S(1)}, f32[256]{0:T(256)}, u32[]{:S(2)}) copy-start(f32[256]{0:T(256)} %param.15) | copy-start | bytes 3076
Sparse Core Ops, SparseCore 0:
  10.7 19.4 all-gather.2
  32.2 75.0 all-gather.4
  109.8 42.6 reduce-scatter.1
where the time goes:
time: 166 us
  waiting for transfers between devices  132 us (80%)
  between operations  13.8 us (8%)
  matrix products  12.8 us (8%)
  local copies, waits for them, and re-layouts  5.16 us (3%)
  other arithmetic  1.86 us (1%)
    all_gather x1, waiting for transfers between devices, body(): lax.all_gather(amplitudes, 'col', axis=1, tiled=True)  77.1 us
    reduce_scatter x1, waiting for transfers between devices, body(): lax.psum_scatter(lax.dot_general(hole_kept, amplitudes, (((0,), (0,)), ((...  45.2 us
    all_gather x1, waiting for transfers between devices, body(): ladder_full = lax.all_gather(ladder_kept, 'row', axis=0, tiled=True)  8.81 us
    dot_general x1, matrix products, body(): lax.dot_general(hole_kept, amplitudes, (((0,), (0,)), ((), ())), preferre...  8.51 us
    dot_general x1, matrix products, body(): jnp.dot(lax.all_gather(amplitudes, 'col', axis=1, tiled=True), ladder_ful...  4.27 us
  transfers between devices with their start and end apart: 3, of which 3 were waited for; matrix products, arithmetic and copies ran while one was open for 6% of the time, Pallas kernels for 0%

commit v1 on v0

--- a/solution.py
+++ b/solution.py
@@ -1,10 +1,278 @@
+import functools
+
 import jax
 import jax.numpy as jnp
 from jax import lax
+from jax.experimental import pallas as pl
+from jax.experimental.pallas import tpu as pltpu
 from jax.sharding import PartitionSpec as P
 
-
-def body(amplitudes, drive, pair_irrep, occ_irrep, ladder_ints, hole_ints, occ_energy, pair_energy):
+MESH = pl.DeviceIdType.MESH
+WIRE = jnp.float32
+CHUNKS = 4
+LINE = 4
+ROWS = 4
+
+
+def kernel(
+    a_ref, drive_ref, pair_ref, occ_ref, ladder_ref, hole_ref, energy_ref, pair_energy_ref,
+    res_ref, upd_ref,
+    zbuf, abuf, wbuf, wout, vbuf, occ_col, energy_col, psend, precv,
+    v_sem, zs_sem, zr_sem, as_sem, ar_sem, ws_sem, wr_sem, wxs_sem, ps_sem, pr_sem,
+):
+    row = lax.axis_index("row")
+    col = lax.axis_index("col")
+    y, core = row // 2, row % 2
+    z, x = col // 2, col % 2
+    occ_rows, pair_cols = a_ref.shape
+    step = occ_rows // CHUNKS
+    sib = y * 2 + 1 - core
+    ynb = (1 - y) * 2 + core
+    diag = (1 - y) * 2 + 1 - core
+    to_sib, to_y = (sib, col), (ynb, col)
+    to_x = (row, z * 2 + 1 - x)
+    to_right, to_left = (row, (z + 1) * 2 + x), (row, (z - 1) * 2 + x)
+
+    def remote(src, dst, ssem, rsem, dev):
+        return pltpu.make_async_remote_copy(
+            src_ref=src, dst_ref=dst, send_sem=ssem, recv_sem=rsem, device_id=dev, device_id_type=MESH
+        )
+
+    def v_copy(rr):
+        return pltpu.make_async_copy(
+            hole_ref.at[:, pl.ds(pl.multiple_of(rr * occ_rows, occ_rows), occ_rows)], vbuf.at[rr], v_sem.at[rr]
+        )
+
+    for rr in (row, sib, ynb, diag):
+        v_copy(rr).start()
+
+    barrier = pltpu.get_barrier_semaphore()
+    for dev in (to_sib, to_y, to_x):
+        pl.semaphore_signal(barrier, inc=1, device_id=dev, device_id_type=MESH)
+
+    @pl.when(z < LINE - 1)
+    def _():
+        pl.semaphore_signal(barrier, inc=1, device_id=to_right, device_id_type=MESH)
+
+    @pl.when(z > 0)
+    def _():
+        pl.semaphore_signal(barrier, inc=1, device_id=to_left, device_id_type=MESH)
+
+    zbuf[z] = a_ref[...]
+    abuf[row] = a_ref[...]
+
+    own_pairs = pair_ref[pl.ds(col, 1), :].astype(jnp.float32)
+    for half in range(2):
+        down = jnp.broadcast_to(
+            pair_ref[pl.ds(row * 2 + half, 1), :].astype(jnp.float32), (pair_cols, pair_cols)
+        ).T
+        block = ladder_ref[half * pair_cols:(half + 1) * pair_cols, :].astype(jnp.float32)
+        wout[half] = jnp.where(down == own_pairs, block, 0.0).astype(jnp.bfloat16)
+    wbuf[row, x] = wout[x]
+
+    pl.semaphore_wait(barrier, 3 + (z > 0).astype(jnp.int32) + (z < LINE - 1).astype(jnp.int32))
+
+    def rows_of(k):
+        return pl.ds(k * step, step)
+
+    def z_copy(right, dist, k):
+        src = z - dist if right else z + dist
+        block = zbuf.at[src, rows_of(k), :]
+        return remote(
+            block, block, zs_sem.at[0 if right else 1, dist, k], zr_sem.at[src, k],
+            to_right if right else to_left,
+        )
+
+    def z_recv(src, k):
+        block = zbuf.at[src, rows_of(k), :]
+        return remote(block, block, zs_sem.at[0, 0, k], zr_sem.at[src, k], to_right)
+
+    def can_send(right, dist):
+        if right:
+            return jnp.logical_and(z - dist >= 0, z < LINE - 1)
+        return jnp.logical_and(z + dist < LINE, z > 0)
+
+    def z_send_own(k):
+        for right in (True, False):
+            @pl.when(can_send(right, 0))
+            def _():
+                z_copy(right, 0, k).start()
+
+    def z_forward(dist, k):
+        for right in (True, False):
+            src = z - dist if right else z + dist
+            here = src >= 0 if right else src < LINE
+
+            @pl.when(here)
+            def _():
+                z_recv(src, k).wait_recv()
+
+            @pl.when(can_send(right, dist))
+            def _():
+                z_copy(right, dist, k).start()
+
+    z_send_own(0)
+
+    w_x = remote(wout.at[1 - x], wbuf.at[row, x], wxs_sem, wr_sem.at[row, x], to_x)
+    w_x.start()
+
+    def w_copy(slot, part, dev, n):
+        block = wbuf.at[slot, part]
+        return remote(block, block, ws_sem.at[n], wr_sem.at[slot, part], dev)
+
+    def a_copy(slot, dev, n):
+        block = abuf.at[slot]
+        return remote(block, block, as_sem.at[n], ar_sem.at[slot], dev)
+
+    w_sends = [
+        w_copy(row, x, to_y, 0), w_copy(row, x, to_sib, 1),
+        w_copy(row, 1 - x, to_y, 2), w_copy(row, 1 - x, to_sib, 3),
+        w_copy(ynb, x, to_sib, 4), w_copy(ynb, 1 - x, to_sib, 5),
+    ]
+    a_sends = [a_copy(row, to_y, 0), a_copy(row, to_sib, 1), a_copy(ynb, to_sib, 2)]
+    w_sends[0].start()
+    w_sends[1].start()
+    a_sends[1].start()
+    a_sends[0].start()
+    z_send_own(1)
+
+    occ_col[...] = jnp.broadcast_to(occ_ref[pl.ds(row, 1), :].astype(jnp.float32), (128, occ_rows)).T
+    nocc = energy_ref.shape[0]
+
+    def hole(rr, first):
+        v_copy(rr).wait()
+
+        @pl.loop(0, CHUNKS)
+        def _(i):
+            rows = pl.ds(pl.multiple_of(i * step, step), step)
+            labels = occ_ref[pl.ds(rr, 1), :].astype(jnp.float32)
+            keep = occ_col[rows, 0:1] == labels
+            block = jnp.where(keep, vbuf[rr, rows, :].astype(jnp.float32), 0.0).astype(jnp.bfloat16)
+            part = jnp.dot(block, abuf[rr], preferred_element_type=jnp.float32)
+            if first:
+                res_ref[rows, :] = drive_ref[rows, :] + part
+            else:
+                res_ref[rows, :] += part
+
+    w_copy(row, 1 - x, to_y, 2).wait_recv()
+    w_sends[2].start()
+    w_sends[3].start()
+    hole(row, True)
+    z_forward(1, 0)
+    w_sends[4].wait_recv()
+    w_sends[4].start()
+    a_copy(sib, to_sib, 1).wait_recv()
+    hole(sib, False)
+    z_forward(2, 0)
+    z_send_own(2)
+    w_sends[5].wait_recv()
+    w_sends[5].start()
+    z_forward(1, 1)
+    a_sends[2].wait_recv()
+    a_sends[2].start()
+    z_forward(3, 0)
+    hole(ynb, False)
+    z_forward(2, 1)
+    z_send_own(3)
+    a_copy(diag, to_sib, 2).wait_recv()
+    hole(diag, False)
+    z_forward(3, 1)
+
+    for slot, part, n in ((sib, x, 1), (sib, 1 - x, 3), (diag, x, 4), (diag, 1 - x, 5)):
+        w_copy(slot, part, to_sib, n).wait_recv()
+
+    def p_copy(k):
+        return remote(psend.at[k], precv.at[k], ps_sem.at[k], pr_sem.at[k], to_x)
+
+    def particle(k):
+        rows = rows_of(k)
+        away = jnp.zeros((step, pair_cols), jnp.float32)
+        for s in range(LINE):
+            away += jnp.dot(zbuf[s, rows, :], wbuf[s, 1 - x], preferred_element_type=jnp.float32)
+        psend[k] = away.astype(WIRE)
+        p_copy(k).start()
+        own = res_ref[rows, :]
+        for s in range(LINE):
+            own += jnp.dot(zbuf[s, rows, :], wbuf[s, x], preferred_element_type=jnp.float32)
+        res_ref[rows, :] = own
+
+    def finish(k):
+        p_copy(k).wait_recv()
+        for i in range(step // nocc):
+            base = k * step + i * nocc
+            rows = pl.ds(base, nocc)
+            total = res_ref[rows, :] + precv[k, pl.ds(i * nocc, nocc), :].astype(jnp.float32)
+            res_ref[rows, :] = total
+            first_energy = energy_ref[row * (occ_rows // nocc) + base // nocc]
+            denominator = pair_energy_ref[...] - (energy_col[:, 0:1] + first_energy)
+            upd_ref[rows, :] = (a_ref[rows, :].astype(jnp.float32) - total / denominator).astype(jnp.bfloat16)
+
+    for i in range(nocc):
+        energy_col[i:i + 1, :] = jnp.full((1, 128), energy_ref[i], jnp.float32)
+
+    for k in range(CHUNKS):
+        if k >= 2:
+            for dist in (1, 2, 3):
+                z_forward(dist, k)
+        particle(k)
+        if k >= 1:
+            finish(k - 1)
+    finish(CHUNKS - 1)
+
+    for k in range(CHUNKS):
+        p_copy(k).wait_send()
+        for dist in range(LINE):
+            for right in (True, False):
+                @pl.when(can_send(right, dist))
+                def _():
+                    z_copy(right, dist, k).wait_send()
+    w_x.wait_send()
+    for copy in w_sends + a_sends:
+        copy.wait_send()
+
+
+def fused(amplitudes, drive, pair_irrep, occ_irrep, ladder_ints, hole_ints, occ_energy, pair_energy):
+    occ_rows, pair_cols = amplitudes.shape
+    step = occ_rows // CHUNKS
+    pairs = pair_irrep.reshape(-1, pair_cols)
+    occs = occ_irrep.reshape(-1, occ_rows)
+    vmem = pl.BlockSpec(memory_space=pltpu.VMEM)
+    dma = pltpu.SemaphoreType.DMA
+    bf16 = jnp.bfloat16
+    return pl.pallas_call(
+        kernel,
+        out_shape=(
+            jax.ShapeDtypeStruct((occ_rows, pair_cols), jnp.float32),
+            jax.ShapeDtypeStruct((occ_rows, pair_cols), bf16),
+        ),
+        in_specs=[vmem, vmem, vmem, vmem, vmem, pl.BlockSpec(memory_space=pl.ANY),
+                  pl.BlockSpec(memory_space=pltpu.SMEM), vmem],
+        out_specs=(vmem, vmem),
+        scratch_shapes=[
+            pltpu.VMEM((LINE, occ_rows, pair_cols), bf16),
+            pltpu.VMEM((ROWS, occ_rows, pair_cols), bf16),
+            pltpu.VMEM((ROWS, 2, pair_cols, pair_cols), bf16),
+            pltpu.VMEM((2, pair_cols, pair_cols), bf16),
+            pltpu.VMEM((ROWS, occ_rows, occ_rows), bf16),
+            pltpu.VMEM((occ_rows, 128), jnp.float32),
+            pltpu.VMEM((occ_energy.shape[0], 128), jnp.float32),
+            pltpu.VMEM((CHUNKS, step, pair_cols), WIRE),
+            pltpu.VMEM((CHUNKS, step, pair_cols), WIRE),
+            dma((ROWS,)),
+            dma((2, LINE, CHUNKS)), dma((LINE, CHUNKS)),
+            dma((3,)), dma((ROWS,)),
+            dma((6,)), dma((ROWS, 2)),
+            dma,
+            dma((CHUNKS,)), dma((CHUNKS,)),
+        ],
+        compiler_params=pltpu.CompilerParams(
+            collective_id=0, has_side_effects=True, vmem_limit_bytes=48 * 2**20
+        ),
+        cost_estimate=pl.CostEstimate(flops=3_300_000_000, bytes_accessed=12_000_000, transcendentals=0),
+    )(amplitudes, drive, pairs, occs, ladder_ints, hole_ints, occ_energy, pair_energy.reshape(1, -1))
+
+
+def general(amplitudes, drive, pair_irrep, occ_irrep, ladder_ints, hole_ints, occ_energy, pair_energy):
     row_rank = lax.axis_index("row")
     col_rank = lax.axis_index("col")
     occ_rows = amplitudes.shape[0]
@@ -25,13 +293,10 @@
     hole_kept = jnp.where(
         own_occ[:, None] == occ_irrep[None, :], hole_ints, jnp.zeros_like(hole_ints)
     )
-    hole_part = lax.psum_scatter(
-        lax.dot_general(
-            hole_kept, amplitudes, (((0,), (0,)), ((), ())), preferred_element_type=jnp.float32
-        ),
-        "row",
-        scatter_dimension=0,
-        tiled=True,
+    hole_part = jnp.dot(
+        hole_kept,
+        lax.all_gather(amplitudes, "row", axis=0, tiled=True),
+        preferred_element_type=jnp.float32,
     )
     residual = drive + particle + hole_part
     pair_occ = (occ_energy[:, None] + occ_energy[None, :]).reshape(-1)
@@ -42,6 +307,7 @@
 
 
 def solution(mesh):
+    body = fused if (mesh.shape["row"], mesh.shape["col"]) == (ROWS, 2 * LINE) else general
     in_specs = (
         P("row", "col"),
         P("row", "col"),

time: 166 us -> 67.5 us (0.41)
  waiting for transfers between devices: 132 us -> 0 us
  Pallas kernels: 0 us -> 58.8 us
  between operations: 13.8 us -> 0.64 us
  matrix products: 12.8 us -> 0 us
  local copies, waits for them, and re-layouts: 5.16 us -> 7.74 us
  other arithmetic: 1.86 us -> 0 us
    all_gather x2 -> x0, waiting for transfers between devices: 85.9 us -> none  [the longest x1 77.1 us: body(): lax.all_gather(amplitudes, 'col', axis=1, tiled=True)]
    pallas_call x0 -> x1, Pallas kernels: none -> 58.8 us  [fused(): pl.pallas_call(kernel, out_shape=(jax.ShapeDtypeStruct((occ_rows, pair_co...]
    reduce_scatter x1 -> x0, waiting for transfers between devices: 45.2 us -> none  [body(): lax.psum_scatter(lax.dot_general(hole_kept, amplitudes, (((0,), (0,)), ((...]
    dot_general x2 -> x0, matrix products: 12.8 us -> none  [the longest x1 8.51 us: body(): lax.dot_general(hole_kept, amplitudes, (((0,), (0,)), ((), ())), preferre...]
    unnamed x12, local copies, waits for them, and re-layouts: 2.86 us -> 6.31 us
    dynamic_slice x4 -> x0, local copies, waits for them, and re-layouts: 2.22 us -> none  [the longest x1 0.76 us: body(): lax.dynamic_slice_in_dim(pair_irrep, row_rank * ladder_rows, ladder_rows)]
    select_n x1 -> x0, other arithmetic: 1.79 us -> none  [body(): jnp.where(ladder_labels[:, None] == own_pairs[None, :], ladder_ints, jnp....]
  transfers between devices with their start and end apart: 3 -> 0, of which waited for: 3 -> 0; matrix products, arithmetic and copies ran while one was open for 6% -> 0% of each run, Pallas kernels for 0% -> 0%
where the time goes in v1:
time: 67.5 us; the launch traced here: 67.2 us
  Pallas kernels  58.8 us (87%)
  local copies, waits for them, and re-layouts  7.74 us (11%)
    pallas_call x1, Pallas kernels, fused(): pl.pallas_call(kernel, out_shape=(jax.ShapeDtypeStruct((occ_rows, pair_co...  58.8 us
    unnamed x12, local copies, waits for them, and re-layouts  6.31 us

profile of v1, /device:TPU:0, one launch (start us, length us, event | category | flops | bytes accessed | tf_op | source)
XLA Modules:
  0.0 67.2 jit_solution(630433829533446500)
XLA Ops:
  0.6 0.7 %reshape.13.pair_ref = s32[8,256]{1,0:T(8,128)S(1)} reshape(s32[2048]{0:T(1024)} %param.10) | data formatting | bytes 16384 | tf_op jit(solution)/shard_map/reshape | solution.py:237
  1.3 0.7 %reshape.14.occ_ref = s32[4,1024]{1,0:T(4,128)S(1)} reshape(s32[4096]{0:T(1024)} %param.11) | data formatting | bytes 32768 | tf_op jit(solution)/shard_map/reshape | solution.py:238
  2.1 0.0 copy-start
  2.1 1.2 %copy-done = f32[1024,256]{1,0:T(8,128)S(1)} copy-done((f32[1024,256]{1,0:T(8,128)S(1)}, f32[1024,256]{1,0:T(8,128)}, u32[]{:S(2)}) %copy-start) | copy-done | bytes 1048600
  3.3 0.0 copy-start.1
  3.3 1.0 %copy-done.1 = bf16[1024,256]{1,0:T(8,128)(2,1)S(1)} copy-done((bf16[1024,256]{1,0:T(8,128)(2,1)S(1)}, bf16[1024,256]{1,0:T(8,128)(2,1)}, u32[]{:S(2)}) %copy-start.1) | copy-done | bytes 524312
  4.3 0.0 copy-start.2
  4.3 0.9 %copy-done.2 = bf16[512,256]{1,0:T(8,128)(2,1)S(1)} copy-done((bf16[512,256]{1,0:T(8,128)(2,1)S(1)}, bf16[512,256]{1,0:T(8,128)(2,1)}, u32[]{:S(2)}) %copy-start.2) | copy-done | bytes 262168
  5.3 0.0 copy-start.3
  5.3 0.7 %copy-done.3 = f32[256]{0:T(256)S(1)} copy-done((f32[256]{0:T(256)S(1)}, f32[256]{0:T(256)}, u32[]{:S(2)}) %copy-start.3) | copy-done | bytes 1048
  6.0 0.0 copy-start.4
  6.0 0.7 copy-done.4
  6.6 58.8 %shard_map.95 = (f32[1024,256]{1,0:T(8,128)S(1)}, bf16[1024,256]{1,0:T(8,128)(2,1)S(1)}) custom-call(bf16[1024,256]{1,0:T(8,128)(2,1)S(1)} %copy-done.1, f32[1024,256]{1,0:T(8,128)S(1)} %copy-done, s32[8,256]{1,0:T(8,128)S(1)} %reshape.13.pair_ref, s32[4,1024]{1,0:T(4,128)S(1)} %reshape.14.occ_ref, bf16[512,256]{1,0:T(8,128)(2,1)S(1)} %copy-done.2, ...), custom_call_target="tpu_custom_call" | custom-call | flops 3300000000 | bytes 12000000 | tf_op jit(solution)/shard_map/pallas_call | solution.py:242
  65.4 1.0 %copy.12 = f32[1024,256]{1,0:T(8,128)} copy(f32[1024,256]{1,0:T(8,128)S(1)} %get-tuple-element.4) | data formatting | bytes 2097152
  66.4 0.8 %copy.13 = bf16[1024,256]{1,0:T(8,128)(2,1)} copy(bf16[1024,256]{1,0:T(8,128)(2,1)S(1)} %get-tuple-element.5) | data formatting | bytes 1048576
Async XLA Ops:
  2.1 1.2 %copy-start = (f32[1024,256]{1,0:T(8,128)S(1)}, f32[1024,256]{1,0:T(8,128)}, u32[]{:S(2)}) copy-start(f32[1024,256]{1,0:T(8,128)} %drive_ref.1) | copy-start | bytes 3145732
  3.3 1.0 %copy-start.1 = (bf16[1024,256]{1,0:T(8,128)(2,1)S(1)}, bf16[1024,256]{1,0:T(8,128)(2,1)}, u32[]{:S(2)}) copy-start(bf16[1024,256]{1,0:T(8,128)(2,1)} %a_ref.1) | copy-start | bytes 1572868
  4.3 0.9 %copy-start.2 = (bf16[512,256]{1,0:T(8,128)(2,1)S(1)}, bf16[512,256]{1,0:T(8,128)(2,1)}, u32[]{:S(2)}) copy-start(bf16[512,256]{1,0:T(8,128)(2,1)} %ladder_ref.1) | copy-start | bytes 786436
  5.3 0.7 %copy-start.3 = (f32[256]{0:T(256)S(1)}, f32[256]{0:T(256)}, u32[]{:S(2)}) copy-start(f32[256]{0:T(256)} %param.15) | copy-start | bytes 3076
  6.0 0.7 copy-start.4

commit v2 on v1

--- a/solution.py
+++ b/solution.py
@@ -9,22 +9,24 @@
 
 MESH = pl.DeviceIdType.MESH
 WIRE = jnp.float32
-CHUNKS = 4
+CHUNKS = 8
+HALF = CHUNKS // 2
 LINE = 4
 ROWS = 4
 
 
 def kernel(
-    a_ref, drive_ref, pair_ref, occ_ref, ladder_ref, hole_ref, energy_ref, pair_energy_ref,
+    a_hbm, drive_hbm, pair_hbm, occ_hbm, ladder_hbm, hole_ref, energy_hbm, pair_energy_hbm,
     res_ref, upd_ref,
     zbuf, abuf, wbuf, wout, vbuf, occ_col, energy_col, psend, precv,
-    v_sem, zs_sem, zr_sem, as_sem, ar_sem, ws_sem, wr_sem, wxs_sem, ps_sem, pr_sem,
+    pair_ref, occ_ref, ladder_ref, energy_ref, pair_energy_ref,
+    v_sem, zs_sem, zr_sem, as_sem, ar_sem, ws_sem, wr_sem, wxs_sem, ps_sem, pr_sem, in_sem,
 ):
     row = lax.axis_index("row")
     col = lax.axis_index("col")
     y, core = row // 2, row % 2
     z, x = col // 2, col % 2
-    occ_rows, pair_cols = a_ref.shape
+    occ_rows, pair_cols = a_hbm.shape
     step = occ_rows // CHUNKS
     sib = y * 2 + 1 - core
     ynb = (1 - y) * 2 + core
@@ -33,6 +35,10 @@
     to_x = (row, z * 2 + 1 - x)
     to_right, to_left = (row, (z + 1) * 2 + x), (row, (z - 1) * 2 + x)
 
+    def labels_of(ref, start, size):
+        start = pl.multiple_of(start, size)
+        return ref[pl.ds(start, size)].astype(jnp.float32).reshape(1, size)
+
     def remote(src, dst, ssem, rsem, dev):
         return pltpu.make_async_remote_copy(
             src_ref=src, dst_ref=dst, send_sem=ssem, recv_sem=rsem, device_id=dev, device_id_type=MESH
@@ -43,6 +49,15 @@
             hole_ref.at[:, pl.ds(pl.multiple_of(rr * occ_rows, occ_rows), occ_rows)], vbuf.at[rr], v_sem.at[rr]
         )
 
+    loads = [
+        pltpu.make_async_copy(src, dst, in_sem.at[n])
+        for n, (src, dst) in enumerate((
+            (a_hbm, zbuf.at[z]), (a_hbm, abuf.at[row]), (ladder_hbm, ladder_ref), (pair_hbm, pair_ref),
+            (occ_hbm, occ_ref), (drive_hbm, res_ref), (energy_hbm, energy_ref), (pair_energy_hbm, pair_energy_ref),
+        ))
+    ]
+    for load in loads:
+        load.start()
     for rr in (row, sib, ynb, diag):
         v_copy(rr).start()
 
@@ -58,18 +73,8 @@
     def _():
         pl.semaphore_signal(barrier, inc=1, device_id=to_left, device_id_type=MESH)
 
-    zbuf[z] = a_ref[...]
-    abuf[row] = a_ref[...]
-
-    own_pairs = pair_ref[pl.ds(col, 1), :].astype(jnp.float32)
-    for half in range(2):
-        down = jnp.broadcast_to(
-            pair_ref[pl.ds(row * 2 + half, 1), :].astype(jnp.float32), (pair_cols, pair_cols)
-        ).T
-        block = ladder_ref[half * pair_cols:(half + 1) * pair_cols, :].astype(jnp.float32)
-        wout[half] = jnp.where(down == own_pairs, block, 0.0).astype(jnp.bfloat16)
-    wbuf[row, x] = wout[x]
-
+    loads[0].wait()
+    loads[1].wait()
     pl.semaphore_wait(barrier, 3 + (z > 0).astype(jnp.int32) + (z < LINE - 1).astype(jnp.int32))
 
     def rows_of(k):
@@ -111,10 +116,8 @@
             def _():
                 z_copy(right, dist, k).start()
 
-    z_send_own(0)
-
-    w_x = remote(wout.at[1 - x], wbuf.at[row, x], wxs_sem, wr_sem.at[row, x], to_x)
-    w_x.start()
+    for k in range(HALF + 2):
+        z_send_own(k)
 
     def w_copy(slot, part, dev, n):
         block = wbuf.at[slot, part]
@@ -130,54 +133,65 @@
         w_copy(ynb, x, to_sib, 4), w_copy(ynb, 1 - x, to_sib, 5),
     ]
     a_sends = [a_copy(row, to_y, 0), a_copy(row, to_sib, 1), a_copy(ynb, to_sib, 2)]
+    a_sends[0].start()
+    a_sends[1].start()
+
+    loads[2].wait()
+    loads[3].wait()
+    own_pairs = labels_of(pair_ref, col * pair_cols, pair_cols)
+    for half in range(2):
+        down = jnp.broadcast_to(
+            labels_of(pair_ref, (row * 2 + half) * pair_cols, pair_cols), (pair_cols, pair_cols)
+        ).T
+        block = ladder_ref[half * pair_cols:(half + 1) * pair_cols, :].astype(jnp.float32)
+        wout[half] = jnp.where(down == own_pairs, block, 0.0).astype(jnp.bfloat16)
+    wbuf[row, x] = wout[x]
+    w_x = remote(wout.at[1 - x], wbuf.at[row, x], wxs_sem, wr_sem.at[row, x], to_x)
+    w_x.start()
     w_sends[0].start()
     w_sends[1].start()
-    a_sends[1].start()
-    a_sends[0].start()
-    z_send_own(1)
-
-    occ_col[...] = jnp.broadcast_to(occ_ref[pl.ds(row, 1), :].astype(jnp.float32), (128, occ_rows)).T
+
+    for load in loads[4:]:
+        load.wait()
+    occ_col[...] = jnp.broadcast_to(labels_of(occ_ref, row * occ_rows, occ_rows), (128, occ_rows)).T
     nocc = energy_ref.shape[0]
 
-    def hole(rr, first):
+    tile = 256
+
+    def hole(rr):
         v_copy(rr).wait()
 
-        @pl.loop(0, CHUNKS)
+        labels = labels_of(occ_ref, rr * occ_rows, occ_rows)
+
+        @pl.loop(0, occ_rows // tile)
         def _(i):
-            rows = pl.ds(pl.multiple_of(i * step, step), step)
-            labels = occ_ref[pl.ds(rr, 1), :].astype(jnp.float32)
+            rows = pl.ds(pl.multiple_of(i * tile, tile), tile)
             keep = occ_col[rows, 0:1] == labels
             block = jnp.where(keep, vbuf[rr, rows, :].astype(jnp.float32), 0.0).astype(jnp.bfloat16)
-            part = jnp.dot(block, abuf[rr], preferred_element_type=jnp.float32)
-            if first:
-                res_ref[rows, :] = drive_ref[rows, :] + part
-            else:
-                res_ref[rows, :] += part
-
+            res_ref[rows, :] += jnp.dot(block, abuf[rr], preferred_element_type=jnp.float32)
+
+    hole(row)
     w_copy(row, 1 - x, to_y, 2).wait_recv()
     w_sends[2].start()
     w_sends[3].start()
-    hole(row, True)
-    z_forward(1, 0)
-    w_sends[4].wait_recv()
-    w_sends[4].start()
+    for k in range(HALF):
+        z_forward(1, k)
     a_copy(sib, to_sib, 1).wait_recv()
-    hole(sib, False)
-    z_forward(2, 0)
-    z_send_own(2)
-    w_sends[5].wait_recv()
-    w_sends[5].start()
-    z_forward(1, 1)
+    hole(sib)
+    for k in range(HALF):
+        z_forward(2, k)
+    for k in range(HALF + 2, CHUNKS):
+        z_send_own(k)
     a_sends[2].wait_recv()
     a_sends[2].start()
-    z_forward(3, 0)
-    hole(ynb, False)
-    z_forward(2, 1)
-    z_send_own(3)
+    hole(ynb)
+    for n in (4, 5):
+        w_sends[n].wait_recv()
+        w_sends[n].start()
     a_copy(diag, to_sib, 2).wait_recv()
-    hole(diag, False)
-    z_forward(3, 1)
-
+    hole(diag)
+    for k in (HALF, HALF + 1):
+        z_forward(1, k)
     for slot, part, n in ((sib, x, 1), (sib, 1 - x, 3), (diag, x, 4), (diag, 1 - x, 5)):
         w_copy(slot, part, to_sib, n).wait_recv()
 
@@ -204,16 +218,18 @@
             total = res_ref[rows, :] + precv[k, pl.ds(i * nocc, nocc), :].astype(jnp.float32)
             res_ref[rows, :] = total
             first_energy = energy_ref[row * (occ_rows // nocc) + base // nocc]
-            denominator = pair_energy_ref[...] - (energy_col[:, 0:1] + first_energy)
-            upd_ref[rows, :] = (a_ref[rows, :].astype(jnp.float32) - total / denominator).astype(jnp.bfloat16)
+            denominator = pair_energy_ref[...].reshape(1, pair_cols) - (energy_col[:, 0:1] + first_energy)
+            upd_ref[rows, :] = (abuf[row, rows, :].astype(jnp.float32) - total / denominator).astype(jnp.bfloat16)
 
     for i in range(nocc):
         energy_col[i:i + 1, :] = jnp.full((1, 128), energy_ref[i], jnp.float32)
 
     for k in range(CHUNKS):
-        if k >= 2:
-            for dist in (1, 2, 3):
-                z_forward(dist, k)
+        if k >= HALF:
+            z_forward(2, k)
+            if k + 2 < CHUNKS:
+                z_forward(1, k + 2)
+        z_forward(3, k)
         particle(k)
         if k >= 1:
             finish(k - 1)
@@ -234,8 +250,6 @@
 def fused(amplitudes, drive, pair_irrep, occ_irrep, ladder_ints, hole_ints, occ_energy, pair_energy):
     occ_rows, pair_cols = amplitudes.shape
     step = occ_rows // CHUNKS
-    pairs = pair_irrep.reshape(-1, pair_cols)
-    occs = occ_irrep.reshape(-1, occ_rows)
     vmem = pl.BlockSpec(memory_space=pltpu.VMEM)
     dma = pltpu.SemaphoreType.DMA
     bf16 = jnp.bfloat16
@@ -245,8 +259,7 @@
             jax.ShapeDtypeStruct((occ_rows, pair_cols), jnp.float32),
             jax.ShapeDtypeStruct((occ_rows, pair_cols), bf16),
         ),
-        in_specs=[vmem, vmem, vmem, vmem, vmem, pl.BlockSpec(memory_space=pl.ANY),
-                  pl.BlockSpec(memory_space=pltpu.SMEM), vmem],
+        in_specs=[pl.BlockSpec(memory_space=pl.ANY)] * 8,
         out_specs=(vmem, vmem),
         scratch_shapes=[
             pltpu.VMEM((LINE, occ_rows, pair_cols), bf16),
@@ -258,18 +271,24 @@
             pltpu.VMEM((occ_energy.shape[0], 128), jnp.float32),
             pltpu.VMEM((CHUNKS, step, pair_cols), WIRE),
             pltpu.VMEM((CHUNKS, step, pair_cols), WIRE),
+            pltpu.VMEM(pair_irrep.shape, jnp.int32),
+            pltpu.VMEM(occ_irrep.shape, jnp.int32),
+            pltpu.VMEM(ladder_ints.shape, bf16),
+            pltpu.SMEM(occ_energy.shape, jnp.float32),
+            pltpu.VMEM(pair_energy.shape, jnp.float32),
             dma((ROWS,)),
             dma((2, LINE, CHUNKS)), dma((LINE, CHUNKS)),
             dma((3,)), dma((ROWS,)),
             dma((6,)), dma((ROWS, 2)),
             dma,
             dma((CHUNKS,)), dma((CHUNKS,)),
+            dma((8,)),
         ],
         compiler_params=pltpu.CompilerParams(
-            collective_id=0, has_side_effects=True, vmem_limit_bytes=48 * 2**20
+            collective_id=0, has_side_effects=True, vmem_limit_bytes=58 * 2**20
         ),
         cost_estimate=pl.CostEstimate(flops=3_300_000_000, bytes_accessed=12_000_000, transcendentals=0),
-    )(amplitudes, drive, pairs, occs, ladder_ints, hole_ints, occ_energy, pair_energy.reshape(1, -1))
+    )(amplitudes, drive, pair_irrep, occ_irrep, ladder_ints, hole_ints, occ_energy, pair_energy)
 
 
 def general(amplitudes, drive, pair_irrep, occ_irrep, ladder_ints, hole_ints, occ_energy, pair_energy):

time: 67.5 us -> 59.6 us (0.88)
  Pallas kernels: 58.8 us -> 54.6 us
  local copies, waits for them, and re-layouts: 7.74 us -> 4.13 us
    pallas_call x1, Pallas kernels: 58.8 us -> 54.6 us  [fused(): pl.pallas_call(kernel, out_shape=(jax.ShapeDtypeStruct((occ_rows, pair_co...]
    unnamed x12 -> x2, local copies, waits for them, and re-layouts: 6.31 us -> 4.13 us
    reshape x2 -> x0, local copies, waits for them, and re-layouts: 1.43 us -> none  [the longest x1 0.73 us: fused(): occs = occ_irrep.reshape(-1, occ_rows)]
where the time goes in v2:
time: 59.6 us; the launch traced here: 59.4 us
  Pallas kernels  54.6 us (92%)
  local copies, waits for them, and re-layouts  4.13 us (7%)
  between operations  0.64 us (1%)
    pallas_call x1, Pallas kernels, fused(): pl.pallas_call(kernel, out_shape=(jax.ShapeDtypeStruct((occ_rows, pair_co...  54.6 us
    unnamed x2, local copies, waits for them, and re-layouts  4.13 us

profile of v2, /device:TPU:0, one launch (start us, length us, event | category | flops | bytes accessed | tf_op | source)
XLA Modules:
  0.0 59.4 jit_solution(8054636969103432156)
XLA Ops:
  0.6 54.6 %shard_map.95 = (f32[1024,256]{1,0:T(8,128)}, bf16[1024,256]{1,0:T(8,128)(2,1)}) custom-call(bf16[1024,256]{1,0:T(8,128)(2,1)} %a_hbm.1, f32[1024,256]{1,0:T(8,128)} %drive_hbm.1, s32[2048]{0:T(1024)} %pair_hbm.1, s32[4096]{0:T(1024)} %occ_hbm.1, bf16[512,256]{1,0:T(8,128)(2,1)} %ladder_hbm.1, bf16[1024,4096]{1,0:T(8,128)(2,1)} %hole_ref.1, f32[64]{0:T(128)} %energy_hbm.1, ...), custom_call_target="tpu_custom_call" | custom-call | flops 3300000000 | bytes 12000000 | tf_op jit(solution)/shard_map/pallas_call | solution.py:256
  55.3 2.3 %copy.12 = f32[1024,256]{1,0:T(8,128)} copy(f32[1024,256]{1,0:T(8,128)} %get-tuple-element.4) | data formatting | bytes 2097152
  57.5 1.9 %copy.13 = bf16[1024,256]{1,0:T(8,128)(2,1)} copy(bf16[1024,256]{1,0:T(8,128)(2,1)} %get-tuple-element.5) | data formatting | bytes 1048576

commit v3 on v2

v3 whole, which is shorter than its diff:
```python
import functools

import jax
import jax.numpy as jnp
from jax import lax
from jax.experimental import pallas as pl
from jax.experimental.pallas import tpu as pltpu
from jax.sharding import PartitionSpec as P

MESH = pl.DeviceIdType.MESH
TAIL = 16
LEVELS = 32000.0
CHUNKS = 8
HALF = CHUNKS // 2
LINE = 4
ROWS = 4


def kernel(
    a_hbm, drive_hbm, pair_hbm, occ_hbm, ladder_hbm, hole_ref, energy_hbm, pair_energy_hbm,
    res_ref, upd_ref,
    zbuf, abuf, wbuf, wout, vbuf, occ_col, energy_col, qsend, qrecv, esend, erecv,
    pair_ref, occ_ref, ladder_ref, energy_ref, pair_energy_ref,
    v_sem, zs_sem, zr_sem, as_sem, ar_sem, ws_sem, wr_sem, wxs_sem, ps_sem, pr_sem, es_sem, er_sem, in_sem,
):
    row = lax.axis_index("row")
    col = lax.axis_index("col")
    y, core = row // 2, row % 2
    z, x = col // 2, col % 2
    occ_rows, pair_cols = a_hbm.shape
    step = occ_rows // CHUNKS
    sib = y * 2 + 1 - core
    ynb = (1 - y) * 2 + core
    diag = (1 - y) * 2 + 1 - core
    to_sib, to_y = (sib, col), (ynb, col)
    to_x = (row, z * 2 + 1 - x)
    middle = jnp.logical_or(z == 1, z == 2)
    end = jnp.logical_not(middle)
    mate, cross = (z // 2) * 2 + 1 - z % 2, 3 - z
    far = 3 - mate
    to_mate, to_cross = (row, mate * 2 + x), (row, cross * 2 + x)

    def labels_of(ref, start, size):
        start = pl.multiple_of(start, size)
        return ref[pl.ds(start, size)].astype(jnp.float32).reshape(1, size)

    def remote(src, dst, ssem, rsem, dev):
        return pltpu.make_async_remote_copy(
            src_ref=src, dst_ref=dst, send_sem=ssem, recv_sem=rsem, device_id=dev, device_id_type=MESH
        )

    def v_copy(rr):
        return pltpu.make_async_copy(
            hole_ref.at[:, pl.ds(pl.multiple_of(rr * occ_rows, occ_rows), occ_rows)], vbuf.at[rr], v_sem.at[rr]
        )

    loads = [
        pltpu.make_async_copy(src, dst, in_sem.at[n])
        for n, (src, dst) in enumerate((
            (a_hbm, zbuf.at[z]), (a_hbm, abuf.at[row]), (ladder_hbm, ladder_ref), (pair_hbm, pair_ref),
            (occ_hbm, occ_ref), (drive_hbm, res_ref), (energy_hbm, energy_ref), (pair_energy_hbm, pair_energy_ref),
        ))
    ]
    for load in loads:
        load.start()
    for rr in (row, sib, ynb, diag):
        v_copy(rr).start()

    barrier = pltpu.get_barrier_semaphore()
    for dev in (to_sib, to_y, to_x, to_mate):
        pl.semaphore_signal(barrier, inc=1, device_id=dev, device_id_type=MESH)

    @pl.when(middle)
    def _():
        pl.semaphore_signal(barrier, inc=1, device_id=to_cross, device_id_type=MESH)

    loads[0].wait()
    loads[1].wait()
    pl.semaphore_wait(barrier, 4 + middle.astype(jnp.int32))

    def rows_of(k):
        return pl.ds(k * step, step)

    def z_copy(src, k, dev, n):
        block = zbuf.at[src, rows_of(k), :]
        return remote(block, block, zs_sem.at[n, k], zr_sem.at[src, k], dev)

    def z_own(k):
        @pl.when(middle)
        def _():
            z_copy(z, k, to_cross, 0).start()

        @pl.when(end)
        def _():
            z_copy(z, k, to_mate, 0).start()

    def z_forward(k):
        z_copy(mate, k, to_cross, 1).wait_recv()
        z_copy(mate, k, to_cross, 1).start()

    for k in range(HALF + 1):
        z_own(k)

    def a_copy(slot, part, dev, n):
        size = occ_rows // 4
        block = abuf.at[slot, pl.ds(part * size, size), :]
        return remote(block, block, as_sem.at[n, part], ar_sem.at[slot, part], dev)

    def w_copy(group, slot, part, dev, n):
        block = wbuf.at[group, slot, part]
        return remote(block, block, ws_sem.at[group, n], wr_sem.at[group, slot, part], dev)

    def w_lift(part, n):
        return remote(wbuf.at[0, row, part], wbuf.at[1, row, part], ws_sem.at[0, n], wr_sem.at[1, row, part], to_mate)

    for part in range(4):
        a_copy(row, part, to_sib, 1).start()
    for part in range(2):
        a_copy(row, part, to_y, 0).start()

    loads[2].wait()
    loads[3].wait()
    own_pairs = labels_of(pair_ref, col * pair_cols, pair_cols)
    for half in range(2):
        down = jnp.broadcast_to(
            labels_of(pair_ref, (row * 2 + half) * pair_cols, pair_cols), (pair_cols, pair_cols)
        ).T
        block = ladder_ref[half * pair_cols:(half + 1) * pair_cols, :].astype(jnp.float32)
        wout[half] = jnp.where(down == own_pairs, block, 0.0).astype(jnp.bfloat16)
    wbuf[0, row, x] = wout[x]
    w_x = remote(wout.at[1 - x], wbuf.at[0, row, x], wxs_sem, wr_sem.at[0, row, x], to_x)
    w_x.start()
    parts = (x, 1 - x)

    def w_share(group, i):
        w_copy(group, row, parts[i], to_y, 3 * i).start()
        w_copy(group, row, parts[i], to_sib, 3 * i + 1).start()

    @pl.when(middle)
    def _():
        w_share(0, 0)

    @pl.when(end)
    def _():
        w_lift(x, 0).start()

    for load in loads[4:]:
        load.wait()
    occ_col[...] = jnp.broadcast_to(labels_of(occ_ref, row * occ_rows, occ_rows), (128, occ_rows)).T
    nocc = energy_ref.shape[0]

    tile = 256

    def hole(rr):
        v_copy(rr).wait()

        labels = labels_of(occ_ref, rr * occ_rows, occ_rows)

        @pl.loop(0, occ_rows // tile)
        def _(i):
            rows = pl.ds(pl.multiple_of(i * tile, tile), tile)
            keep = occ_col[rows, 0:1] == labels
            block = jnp.where(keep, vbuf[rr, rows, :].astype(jnp.float32), 0.0).astype(jnp.bfloat16)
            res_ref[rows, :] += jnp.dot(block, abuf[rr], preferred_element_type=jnp.float32)

    w_copy(0, row, 1 - x, to_y, 3).wait_recv()

    @pl.when(middle)
    def _():
        w_share(0, 1)

    @pl.when(end)
    def _():
        w_lift(1 - x, 1).start()

    hole(row)

    @pl.when(middle)
    def _():
        for i in range(2):
            w_copy(1, row, parts[i], to_y, 3 * i).wait_recv()
            w_share(1, i)
        for k in range(HALF):
            z_forward(k)

    for k in range(HALF + 1, CHUNKS):
        z_own(k)
    for part in range(2, 4):
        a_copy(row, part, to_y, 0).start()
    for part in range(4):
        a_copy(sib, part, to_sib, 1).wait_recv()
    hole(sib)

    @pl.when(middle)
    def _():
        for group in range(2):
            for i in range(2):
                w_copy(group, ynb, parts[i], to_sib, 3 * i + 2).wait_recv()
                w_copy(group, ynb, parts[i], to_sib, 3 * i + 2).start()
        for k in range(HALF, CHUNKS):
            z_forward(k)
        for group in range(2):
            for i in range(2):
                w_copy(group, sib, parts[i], to_sib, 3 * i + 1).wait_recv()
                w_copy(group, diag, parts[i], to_sib, 3 * i + 2).wait_recv()

    def encode(ref, total):
        most = jnp.max(jnp.abs(total), axis=0, keepdims=True)
        power = jnp.ceil(jnp.log2(jnp.maximum(most, 1e-30)))
        scaled = total * (LEVELS * jnp.exp2(-power))
        ref[0:step, :] = jnp.floor(scaled + 0.5).astype(jnp.int32).astype(jnp.int16)
        ref[step:step + TAIL, :] = jnp.broadcast_to(power, (TAIL, pair_cols)).astype(jnp.int32).astype(jnp.int16)

    def decode(ref, start, size):
        power = ref[step:step + TAIL, :].astype(jnp.int32).astype(jnp.float32)[0:1, :]
        block = ref[start:start + size, :].astype(jnp.int32).astype(jnp.float32)
        return block * (jnp.exp2(power) * (1.0 / LEVELS))

    def q_copy(k):
        return remote(qsend.at[k], qrecv.at[k], ps_sem.at[k], pr_sem.at[k], to_x)

    def q_pass(k):
        return remote(erecv.at[k, 1 - x], qrecv.at[k], ps_sem.at[k], pr_sem.at[k], to_x)

    def e_copy(k, part):
        return remote(esend.at[k, part], erecv.at[k, part], es_sem.at[k, part], er_sem.at[k, part], to_mate)

    def product(k, group, part):
        rows = rows_of(k)
        total = jnp.zeros((step, pair_cols), jnp.float32)
        for s in range(LINE):
            total += jnp.dot(zbuf[s, rows, :], wbuf[group, s, part], preferred_element_type=jnp.float32)
        return total

    def particle(k):
        rows = rows_of(k)

        @pl.when(middle)
        def _():
            z_copy(cross, k, to_cross, 0).wait_recv()
            z_copy(far, k, to_cross, 1).wait_recv()
            for part in (1 - x, x):
                encode(esend.at[k, part], product(k, 1, part))
                e_copy(k, part).start()
            encode(qsend.at[k], product(k, 0, 1 - x))
            q_copy(k).start()
            res_ref[rows, :] += product(k, 0, x)

        @pl.when(end)
        def _():
            e_copy(k, 1 - x).wait_recv()
            q_pass(k).start()
            e_copy(k, x).wait_recv()
            res_ref[rows, :] += decode(erecv.at[k, x], 0, step)

    def finish(k):
        q_copy(k).wait_recv()
        for i in range(step // nocc):
            base = k * step + i * nocc
            rows = pl.ds(base, nocc)
            total = res_ref[rows, :] + decode(qrecv.at[k], i * nocc, nocc)
            res_ref[rows, :] = total
            first_energy = energy_ref[row * (occ_rows // nocc) + base // nocc]
            denominator = pair_energy_ref[...].reshape(1, pair_cols) - (energy_col[:, 0:1] + first_energy)
            upd_ref[rows, :] = (abuf[row, rows, :].astype(jnp.float32) - total / denominator).astype(jnp.bfloat16)

    for i in range(nocc):
        energy_col[i:i + 1, :] = jnp.full((1, 128), energy_ref[i], jnp.float32)

    for k in range(CHUNKS):
        particle(k)
        if k == 1:
            for part in range(4):
                a_copy(ynb, part, to_sib, 2).wait_recv()
                a_copy(ynb, part, to_sib, 2).start()
            hole(ynb)
        if k == 3:
            for part in range(4):
                a_copy(diag, part, to_sib, 2).wait_recv()
            hole(diag)
        if k >= 4:
            finish(k - 4)
    for k in range(CHUNKS - 4, CHUNKS):
        finish(k)

    for part in range(4):
        a_copy(row, part, to_y, 0).wait_send()
        a_copy(row, part, to_sib, 1).wait_send()
        a_copy(ynb, part, to_sib, 2).wait_send()
    w_x.wait_send()

    @pl.when(middle)
    def _():
        for k in range(CHUNKS):
            z_copy(z, k, to_cross, 0).wait_send()
            z_copy(mate, k, to_cross, 1).wait_send()
            q_copy(k).wait_send()
            for part in range(2):
                e_copy(k, part).wait_send()
        for group in range(2):
            for i in range(2):
                w_copy(group, row, parts[i], to_y, 3 * i).wait_send()
                w_copy(group, row, parts[i], to_sib, 3 * i + 1).wait_send()
                w_copy(group, ynb, parts[i], to_sib, 3 * i + 2).wait_send()

    @pl.when(end)
    def _():
        for k in range(CHUNKS):
            z_copy(z, k, to_mate, 0).wait_send()
            q_pass(k).wait_send()
        w_lift(x, 0).wait_send()
        w_lift(1 - x, 1).wait_send()


def fused(amplitudes, drive, pair_irrep, occ_irrep, ladder_ints, hole_ints, occ_energy, pair_energy):
    occ_rows, pair_cols = amplitudes.shape
    step = occ_rows // CHUNKS
    vmem = pl.BlockSpec(memory_space=pltpu.VMEM)
    dma = pltpu.SemaphoreType.DMA
    bf16 = jnp.bfloat16
    return pl.pallas_call(
        kernel,
        out_shape=(
            jax.ShapeDtypeStruct((occ_rows, pair_cols), jnp.float32),
            jax.ShapeDtypeStruct((occ_rows, pair_cols), bf16),
        ),
        in_specs=[pl.BlockSpec(memory_space=pl.ANY)] * 8,
        out_specs=(vmem, vmem),
        scratch_shapes=[
            pltpu.VMEM((LINE, occ_rows, pair_cols), bf16),
            pltpu.VMEM((ROWS, occ_rows, pair_cols), bf16),
            pltpu.VMEM((2, ROWS, 2, pair_cols, pair_cols), bf16),
            pltpu.VMEM((2, pair_cols, pair_cols), bf16),
            pltpu.VMEM((ROWS, occ_rows, occ_rows), bf16),
            pltpu.VMEM((occ_rows, 128), jnp.float32),
            pltpu.VMEM((occ_energy.shape[0], 128), jnp.float32),
            pltpu.VMEM((CHUNKS, step + TAIL, pair_cols), jnp.int16),
            pltpu.VMEM((CHUNKS, step + TAIL, pair_cols), jnp.int16),
            pltpu.VMEM((CHUNKS, 2, step + TAIL, pair_cols), jnp.int16),
            pltpu.VMEM((CHUNKS, 2, step + TAIL, pair_cols), jnp.int16),
            pltpu.VMEM(pair_irrep.shape, jnp.int32),
            pltpu.VMEM(occ_irrep.shape, jnp.int32),
            pltpu.VMEM(ladder_ints.shape, bf16),
            pltpu.SMEM(occ_energy.shape, jnp.float32),
            pltpu.VMEM(pair_energy.shape, jnp.float32),
            dma((ROWS,)),
            dma((2, CHUNKS)), dma((LINE, CHUNKS)),
            dma((3, 4)), dma((ROWS, 4)),
            dma((2, 6)), dma((2, ROWS, 2)),
            dma,
            dma((CHUNKS,)), dma((CHUNKS,)),
            dma((CHUNKS, 2)), dma((CHUNKS, 2)),
            dma((8,)),
        ],
        compiler_params=pltpu.CompilerParams(
            collective_id=0, has_side_effects=True, vmem_limit_bytes=58 * 2**20
        ),
        cost_estimate=pl.CostEstimate(flops=3_300_000_000, bytes_accessed=12_000_000, transcendentals=0),
    )(amplitudes, drive, pair_irrep, occ_irrep, ladder_ints, hole_ints, occ_energy, pair_energy)


def general(amplitudes, drive, pair_irrep, occ_irrep, ladder_ints, hole_ints, occ_energy, pair_energy):
    row_rank = lax.axis_index("row")
    col_rank = lax.axis_index("col")
    occ_rows = amplitudes.shape[0]
    pair_cols = amplitudes.shape[1]
    ladder_rows = ladder_ints.shape[0]
    own_pairs = lax.dynamic_slice_in_dim(pair_irrep, col_rank * pair_cols, pair_cols)
    ladder_labels = lax.dynamic_slice_in_dim(pair_irrep, row_rank * ladder_rows, ladder_rows)
    own_occ = lax.dynamic_slice_in_dim(occ_irrep, row_rank * occ_rows, occ_rows)
    ladder_kept = jnp.where(
        ladder_labels[:, None] == own_pairs[None, :], ladder_ints, jnp.zeros_like(ladder_ints)
    )
    ladder_full = lax.all_gather(ladder_kept, "row", axis=0, tiled=True)
    particle = jnp.dot(
        lax.all_gather(amplitudes, "col", axis=1, tiled=True),
        ladder_full,
        preferred_element_type=jnp.float32,
    )
    hole_kept = jnp.where(
        own_occ[:, None] == occ_irrep[None, :], hole_ints, jnp.zeros_like(hole_ints)
    )
    hole_part = jnp.dot(
        hole_kept,
        lax.all_gather(amplitudes, "row", axis=0, tiled=True),
        preferred_element_type=jnp.float32,
    )
    residual = drive + particle + hole_part
    pair_occ = (occ_energy[:, None] + occ_energy[None, :]).reshape(-1)
    own_energy = lax.dynamic_slice_in_dim(pair_occ, row_rank * occ_rows, occ_rows)
    denominator = pair_energy[None, :] - own_energy[:, None]
    updated = (amplitudes.astype(jnp.float32) - residual / denominator).astype(jnp.bfloat16)
    return (residual, updated)


def solution(mesh):
    body = fused if (mesh.shape["row"], mesh.shape["col"]) == (ROWS, 2 * LINE) else general
    in_specs = (
        P("row", "col"),
        P("row", "col"),
        P(),
        P(),
        P("row", "col"),
        P("row", None),
        P(),
        P("col"),
    )
    out_specs = (P("row", "col"), P("row", "col"))
    return jax.shard_map(body, mesh=mesh, in_specs=in_specs, out_specs=out_specs, check_vma=False)
```

time: 59.6 us -> 62.2 us (1.044)
  Pallas kernels: 54.6 us -> 57.2 us
    pallas_call x1, Pallas kernels: 54.6 us -> 57.2 us  [fused(): pl.pallas_call(kernel, out_shape=(jax.ShapeDtypeStruct((occ_rows, pair_co...]
where the time goes in v3:
time: 62.2 us; the launch traced here: 62 us
  Pallas kernels  57.2 us (92%)
  local copies, waits for them, and re-layouts  4.13 us (7%)
  between operations  0.64 us (1%)
    pallas_call x1, Pallas kernels, fused(): pl.pallas_call(kernel, out_shape=(jax.ShapeDtypeStruct((occ_rows, pair_co...  57.2 us
    unnamed x2, local copies, waits for them, and re-layouts  4.13 us

profile of v3, /device:TPU:0, one launch (start us, length us, event | category | flops | bytes accessed | tf_op | source)
XLA Modules:
  0.0 62.0 jit_solution(14066567634888200575)
XLA Ops:
  0.6 57.2 %shard_map.95 = (f32[1024,256]{1,0:T(8,128)}, bf16[1024,256]{1,0:T(8,128)(2,1)}) custom-call(bf16[1024,256]{1,0:T(8,128)(2,1)} %a_hbm.1, f32[1024,256]{1,0:T(8,128)} %drive_hbm.1, s32[2048]{0:T(1024)} %pair_hbm.1, s32[4096]{0:T(1024)} %occ_hbm.1, bf16[512,256]{1,0:T(8,128)(2,1)} %ladder_hbm.1, bf16[1024,4096]{1,0:T(8,128)(2,1)} %hole_ref.1, f32[64]{0:T(128)} %energy_hbm.1, ...), custom_call_target="tpu_custom_call" | custom-call | flops 3300000000 | bytes 12000000 | tf_op jit(solution)/shard_map/pallas_call | solution.py:321
  57.8 2.3 %copy.12 = f32[1024,256]{1,0:T(8,128)} copy(f32[1024,256]{1,0:T(8,128)} %get-tuple-element.4) | data formatting | bytes 2097152
  60.1 1.9 %copy.13 = bf16[1024,256]{1,0:T(8,128)(2,1)} copy(bf16[1024,256]{1,0:T(8,128)(2,1)} %get-tuple-element.5) | data formatting | bytes 1048576

commit v4 on v3

--- a/solution.py
+++ b/solution.py
@@ -12,6 +12,7 @@
 LEVELS = 32000.0
 CHUNKS = 8
 HALF = CHUNKS // 2
+WHOLE = 2
 LINE = 4
 ROWS = 4
 
@@ -85,21 +86,21 @@
         block = zbuf.at[src, rows_of(k), :]
         return remote(block, block, zs_sem.at[n, k], zr_sem.at[src, k], dev)
 
-    def z_own(k):
-        @pl.when(middle)
-        def _():
-            z_copy(z, k, to_cross, 0).start()
-
-        @pl.when(end)
-        def _():
-            z_copy(z, k, to_mate, 0).start()
-
     def z_forward(k):
         z_copy(mate, k, to_cross, 1).wait_recv()
         z_copy(mate, k, to_cross, 1).start()
 
-    for k in range(HALF + 1):
-        z_own(k)
+    @pl.when(middle)
+    def _():
+        for k in range(HALF + 1):
+            z_copy(z, k, to_cross, 0).start()
+        for k in range(WHOLE):
+            z_copy(z, k, to_mate, 2).start()
+
+    @pl.when(end)
+    def _():
+        for k in range(2):
+            z_copy(z, k, to_mate, 0).start()
 
     def a_copy(slot, part, dev, n):
         size = occ_rows // 4
@@ -110,14 +111,11 @@
         block = wbuf.at[group, slot, part]
         return remote(block, block, ws_sem.at[group, n], wr_sem.at[group, slot, part], dev)
 
-    def w_lift(part, n):
-        return remote(wbuf.at[0, row, part], wbuf.at[1, row, part], ws_sem.at[0, n], wr_sem.at[1, row, part], to_mate)
+    def w_lift(slot, part, n):
+        return remote(wbuf.at[0, slot, part], wbuf.at[1, slot, part], ws_sem.at[1, n], wr_sem.at[1, slot, part], to_mate)
 
     for part in range(4):
         a_copy(row, part, to_sib, 1).start()
-    for part in range(2):
-        a_copy(row, part, to_y, 0).start()
-
     loads[2].wait()
     loads[3].wait()
     own_pairs = labels_of(pair_ref, col * pair_cols, pair_cols)
@@ -136,13 +134,14 @@
         w_copy(group, row, parts[i], to_y, 3 * i).start()
         w_copy(group, row, parts[i], to_sib, 3 * i + 1).start()
 
-    @pl.when(middle)
-    def _():
-        w_share(0, 0)
+    w_share(0, 0)
+    a_copy(row, 0, to_y, 0).start()
 
     @pl.when(end)
     def _():
-        w_lift(x, 0).start()
+        w_lift(row, x, 0).start()
+        for k in range(2, 4):
+            z_copy(z, k, to_mate, 0).start()
 
     for load in loads[4:]:
         load.wait()
@@ -159,50 +158,69 @@
         @pl.loop(0, occ_rows // tile)
         def _(i):
             rows = pl.ds(pl.multiple_of(i * tile, tile), tile)
-            keep = occ_col[rows, 0:1] == labels
-            block = jnp.where(keep, vbuf[rr, rows, :].astype(jnp.float32), 0.0).astype(jnp.bfloat16)
+            keep = occ_col[rows, 0:1].astype(jnp.bfloat16) == labels.astype(jnp.bfloat16)
+            block = jnp.where(keep, vbuf[rr, rows, :], jnp.zeros((), jnp.bfloat16))
             res_ref[rows, :] += jnp.dot(block, abuf[rr], preferred_element_type=jnp.float32)
 
     w_copy(0, row, 1 - x, to_y, 3).wait_recv()
-
-    @pl.when(middle)
-    def _():
-        w_share(0, 1)
+    w_share(0, 1)
+    for part in range(1, 4):
+        a_copy(row, part, to_y, 0).start()
 
     @pl.when(end)
     def _():
-        w_lift(1 - x, 1).start()
+        w_lift(row, 1 - x, 1).start()
 
     hole(row)
 
     @pl.when(middle)
     def _():
-        for i in range(2):
-            w_copy(1, row, parts[i], to_y, 3 * i).wait_recv()
-            w_share(1, i)
         for k in range(HALF):
             z_forward(k)
-
-    for k in range(HALF + 1, CHUNKS):
-        z_own(k)
-    for part in range(2, 4):
-        a_copy(row, part, to_y, 0).start()
+        for k in range(WHOLE):
+            z_copy(cross, k, to_mate, 3).wait_recv()
+            z_copy(cross, k, to_mate, 3).start()
+        for k in range(HALF + 1, CHUNKS):
+            z_copy(z, k, to_cross, 0).start()
+
+    for i in range(2):
+        w_copy(0, ynb, parts[i], to_sib, 3 * i + 2).wait_recv()
+        w_copy(0, ynb, parts[i], to_sib, 3 * i + 2).start()
+
+    @pl.when(end)
+    def _():
+        for i in range(2):
+            w_lift(ynb, parts[i], 2 + i).start()
+        for k in range(4, CHUNKS):
+            z_copy(z, k, to_mate, 0).start()
+
+    @pl.when(middle)
+    def _():
+        for i in range(2):
+            w_copy(1, row, parts[i], to_sib, i).wait_recv()
+            w_copy(1, row, parts[i], to_sib, i).start()
+
     for part in range(4):
         a_copy(sib, part, to_sib, 1).wait_recv()
     hole(sib)
 
     @pl.when(middle)
     def _():
-        for group in range(2):
+        for k in range(WHOLE):
+            z_copy(far, k, to_mate, 4).wait_recv()
+            z_copy(far, k, to_mate, 4).start()
+
+    for i in range(2):
+        w_copy(0, sib, parts[i], to_sib, 3 * i + 1).wait_recv()
+        w_copy(0, diag, parts[i], to_sib, 3 * i + 2).wait_recv()
+
+    def w_rest():
+        for i in range(2):
+            w_copy(1, ynb, parts[i], to_sib, 2 + i).wait_recv()
+            w_copy(1, ynb, parts[i], to_sib, 2 + i).start()
+        for slot, n in ((sib, 0), (diag, 2)):
             for i in range(2):
-                w_copy(group, ynb, parts[i], to_sib, 3 * i + 2).wait_recv()
-                w_copy(group, ynb, parts[i], to_sib, 3 * i + 2).start()
-        for k in range(HALF, CHUNKS):
-            z_forward(k)
-        for group in range(2):
-            for i in range(2):
-                w_copy(group, sib, parts[i], to_sib, 3 * i + 1).wait_recv()
-                w_copy(group, diag, parts[i], to_sib, 3 * i + 2).wait_recv()
+                w_copy(1, slot, parts[i], to_sib, n + i).wait_recv()
 
     def encode(ref, total):
         most = jnp.max(jnp.abs(total), axis=0, keepdims=True)
@@ -235,23 +253,32 @@
     def particle(k):
         rows = rows_of(k)
 
-        @pl.when(middle)
-        def _():
-            z_copy(cross, k, to_cross, 0).wait_recv()
-            z_copy(far, k, to_cross, 1).wait_recv()
-            for part in (1 - x, x):
-                encode(esend.at[k, part], product(k, 1, part))
-                e_copy(k, part).start()
+        def share():
             encode(qsend.at[k], product(k, 0, 1 - x))
             q_copy(k).start()
             res_ref[rows, :] += product(k, 0, x)
 
+        @pl.when(middle)
+        def _():
+            if k >= WHOLE:
+                z_copy(cross, k, to_cross, 0).wait_recv()
+                z_copy(far, k, to_cross, 1).wait_recv()
+                for part in (1 - x, x):
+                    encode(esend.at[k, part], product(k, 1, part))
+                    e_copy(k, part).start()
+            share()
+
         @pl.when(end)
         def _():
-            e_copy(k, 1 - x).wait_recv()
-            q_pass(k).start()
-            e_copy(k, x).wait_recv()
-            res_ref[rows, :] += decode(erecv.at[k, x], 0, step)
+            if k < WHOLE:
+                for src in (mate, far, 3 - z):
+                    z_copy(src, k, to_mate, 0).wait_recv()
+                share()
+            else:
+                e_copy(k, 1 - x).wait_recv()
+                q_pass(k).start()
+                e_copy(k, x).wait_recv()
+                res_ref[rows, :] += decode(erecv.at[k, x], 0, step)
 
     def finish(k):
         q_copy(k).wait_recv()
@@ -268,13 +295,20 @@
         energy_col[i:i + 1, :] = jnp.full((1, 128), energy_ref[i], jnp.float32)
 
     for k in range(CHUNKS):
+        @pl.when(middle)
+        def _():
+            if k == WHOLE:
+                w_rest()
+            if 2 <= k < 6:
+                z_forward(HALF + k - 2)
+
         particle(k)
-        if k == 1:
+        if k == 3:
             for part in range(4):
                 a_copy(ynb, part, to_sib, 2).wait_recv()
                 a_copy(ynb, part, to_sib, 2).start()
             hole(ynb)
-        if k == 3:
+        if k == 4:
             for part in range(4):
                 a_copy(diag, part, to_sib, 2).wait_recv()
             hole(diag)
@@ -289,27 +323,29 @@
         a_copy(ynb, part, to_sib, 2).wait_send()
     w_x.wait_send()
 
+    for k in range(CHUNKS):
+        q_copy(k).wait_send()
+    for i in range(2):
+        w_copy(0, row, parts[i], to_y, 3 * i).wait_send()
+        w_copy(0, row, parts[i], to_sib, 3 * i + 1).wait_send()
+        w_copy(0, ynb, parts[i], to_sib, 3 * i + 2).wait_send()
+
+    for n in range(4):
+        w_copy(1, row, x, to_sib, n).wait_send()
+
+    for k in range(CHUNKS):
+        z_copy(z, k, to_mate, 0).wait_send()
+
     @pl.when(middle)
     def _():
         for k in range(CHUNKS):
-            z_copy(z, k, to_cross, 0).wait_send()
             z_copy(mate, k, to_cross, 1).wait_send()
-            q_copy(k).wait_send()
+        for k in range(WHOLE):
+            for n, src in ((2, z), (3, cross), (4, far)):
+                z_copy(src, k, to_mate, n).wait_send()
+        for k in range(WHOLE, CHUNKS):
             for part in range(2):
                 e_copy(k, part).wait_send()
-        for group in range(2):
-            for i in range(2):
-                w_copy(group, row, parts[i], to_y, 3 * i).wait_send()
-                w_copy(group, row, parts[i], to_sib, 3 * i + 1).wait_send()
-                w_copy(group, ynb, parts[i], to_sib, 3 * i + 2).wait_send()
-
-    @pl.when(end)
-    def _():
-        for k in range(CHUNKS):
-            z_copy(z, k, to_mate, 0).wait_send()
-            q_pass(k).wait_send()
-        w_lift(x, 0).wait_send()
-        w_lift(1 - x, 1).wait_send()
 
 
 def fused(amplitudes, drive, pair_irrep, occ_irrep, ladder_ints, hole_ints, occ_energy, pair_energy):
@@ -344,7 +380,7 @@
             pltpu.SMEM(occ_energy.shape, jnp.float32),
             pltpu.VMEM(pair_energy.shape, jnp.float32),
             dma((ROWS,)),
-            dma((2, CHUNKS)), dma((LINE, CHUNKS)),
+            dma((5, CHUNKS)), dma((LINE, CHUNKS)),
             dma((3, 4)), dma((ROWS, 4)),
             dma((2, 6)), dma((2, ROWS, 2)),
             dma,

time: 62.2 us -> 56.5 us (0.908)
  Pallas kernels: 57.2 us -> 51.5 us
    pallas_call x1, Pallas kernels: 57.2 us -> 51.5 us  [fused(): pl.pallas_call(kernel, out_shape=(jax.ShapeDtypeStruct((occ_rows, pair_co...]
where the time goes in v4:
time: 56.5 us; the launch traced here: 56.3 us
  Pallas kernels  51.5 us (91%)
  local copies, waits for them, and re-layouts  4.13 us (7%)
  between operations  0.64 us (1%)
    pallas_call x1, Pallas kernels, fused(): pl.pallas_call(kernel, out_shape=(jax.ShapeDtypeStruct((occ_rows, pair_co...  51.5 us
    unnamed x2, local copies, waits for them, and re-layouts  4.13 us

profile of v4, /device:TPU:0, one launch (start us, length us, event | category | flops | bytes accessed | tf_op | source)
XLA Modules:
  0.0 56.3 jit_solution(419920823921936717)
XLA Ops:
  0.6 51.5 %shard_map.95 = (f32[1024,256]{1,0:T(8,128)}, bf16[1024,256]{1,0:T(8,128)(2,1)}) custom-call(bf16[1024,256]{1,0:T(8,128)(2,1)} %a_hbm.1, f32[1024,256]{1,0:T(8,128)} %drive_hbm.1, s32[2048]{0:T(1024)} %pair_hbm.1, s32[4096]{0:T(1024)} %occ_hbm.1, bf16[512,256]{1,0:T(8,128)(2,1)} %ladder_hbm.1, bf16[1024,4096]{1,0:T(8,128)(2,1)} %hole_ref.1, f32[64]{0:T(128)} %energy_hbm.1, ...), custom_call_target="tpu_custom_call" | custom-call | flops 3300000000 | bytes 12000000 | tf_op jit(solution)/shard_map/pallas_call | solution.py:357
  52.1 2.3 %copy.12 = f32[1024,256]{1,0:T(8,128)} copy(f32[1024,256]{1,0:T(8,128)} %get-tuple-element.4) | data formatting | bytes 2097152
  54.4 1.9 %copy.13 = bf16[1024,256]{1,0:T(8,128)(2,1)} copy(bf16[1024,256]{1,0:T(8,128)(2,1)} %get-tuple-element.5) | data formatting | bytes 1048576
